TPU v7x, 32 devices: a whole 2x2x4 slice. The times are simulated.
32 devices in a mesh: seq: 8 (over z, y), head: 4 (over x, core).
Axes of the slice: x: 2, y: 2, z: 4, core: 2. Of those that a mesh axis runs over, the one named last changes fastest.
Arguments:
- queries: bfloat16 [2048, 2048], P('seq', 'head'), parts along dimension 1, may hold values from -6 to 6
- keys: bfloat16 [2048, 512], P('seq', 'head'), parts along dimension 1, may hold values from -6 to 6
- values: bfloat16 [2048, 512], P('seq', 'head'), parts along dimension 1, may hold values from -6 to 6
- grad_out: bfloat16 [2048, 2048], P('seq', 'head'), parts along dimension 1, may hold values from -6 to 6
- lengths: int32 [16], replicated, may hold values from 1 to 512, 2048 in all
- send_order: int32 [8, 256], replicated, may hold values from 0 to 255, each once within a row
Outputs:
- attended: float32 [2048, 2048], P('seq', 'head'), parts along dimension 1
- grad_queries: float32 [2048, 2048], P('seq', 'head'), parts along dimension 1
- grad_keys: float32 [2048, 512], P('seq', 'head'), parts along dimension 1
- grad_values: float32 [2048, 512], P('seq', 'head'), parts along dimension 1
There are 4 independent parts, one for each index of `head`. A program takes and returns all parts, laid end to end along the dimension named above; an argument that names none is the same for every part. Nothing has to cross between parts.
Inputs may be any that keep to these rules, and one draw needn't show every extreme that they name: `lengths`: they sum to 2048; the longest is exactly 512. `send_order`: each row is a permutation of 0 to 255.
All inputs are finite; a program needn't handle non-finite values.
Results may differ from a plain program's by a relative error of at most 0.039.
Values may be sent and summed in bfloat16 or wider, within the bound.
A program may use at most 64 MiB of HBM per device.

v0:
```python
import math

import jax
import jax.numpy as jnp
from jax import lax
from jax.sharding import PartitionSpec as P

masked_value = -1e30


def doc_index(positions, bounds):
    return jnp.sum((positions[:, None] >= bounds[None, :]).astype(jnp.int32), axis=1)


def visible(query_pos, query_doc, key_pos, bounds):
    key_doc = doc_index(key_pos, bounds)
    return ((query_doc[:, None] == key_doc[None, :]) & (key_pos[None, :] <= query_pos[:, None]))[
        :, None, :
    ]


def block_scores(query_heads, key_block, allowed, score_scale):
    products = (
        jnp.einsum("bhd,td->bht", query_heads, key_block, preferred_element_type=jnp.float32)
        * score_scale
    )
    return jnp.where(allowed, products, masked_value)


def key_blocks(key_piece, value_piece):
    piece_rows = key_piece.shape[0]
    block_rows = math.gcd(piece_rows, 512)
    block_count = piece_rows // block_rows
    offsets = block_rows * jnp.arange(block_count, dtype=jnp.int32)
    stacked = (
        key_piece.reshape(block_count, block_rows, key_piece.shape[1]),
        value_piece.reshape(block_count, block_rows, value_piece.shape[1]),
        offsets,
    )
    return (stacked, block_rows)


def forward_piece(run_state, key_piece, value_piece, context):
    query_heads, query_pos, query_doc, bounds, score_scale = context
    stacked, block_rows = key_blocks(key_piece, value_piece)

    def forward_update(loop_state, block_item):
        run_max, run_total, weighted = loop_state
        key_block, value_block, offset = block_item
        allowed = visible(
            query_pos, query_doc, offset + jnp.arange(block_rows, dtype=jnp.int32), bounds
        )
        scores = block_scores(query_heads, key_block, allowed, score_scale)
        new_max = jnp.maximum(run_max, jnp.max(scores, axis=2))
        exp_weights = jnp.where(allowed, jnp.exp(scores - new_max[:, :, None]), 0.0)
        rescale = jnp.exp(run_max - new_max)
        run_total = run_total * rescale + jnp.sum(exp_weights, axis=2)
        weighted = weighted * rescale[:, :, None] + jnp.einsum(
            "bht,td->bhd",
            exp_weights.astype(jnp.bfloat16),
            value_block,
            preferred_element_type=jnp.float32,
        )
        return ((new_max, run_total, weighted), None)

    run_state, _ = lax.scan(forward_update, run_state, stacked)
    return run_state


def backward_piece(key_piece, value_piece, context):
    query_heads, grad_heads, query_pos, query_doc, bounds, score_scale, log_total, out_dot = context
    stacked, block_rows = key_blocks(key_piece, value_piece)

    def backward_update(query_sum, block_item):
        key_block, value_block, offset = block_item
        allowed = visible(
            query_pos, query_doc, offset + jnp.arange(block_rows, dtype=jnp.int32), bounds
        )
        scores = block_scores(query_heads, key_block, allowed, score_scale)
        weights = jnp.where(allowed, jnp.exp(scores - log_total[:, :, None]), 0.0)
        grad_dots = jnp.einsum(
            "bhd,td->bht", grad_heads, value_block, preferred_element_type=jnp.float32
        )
        score_grads = (weights * (grad_dots - out_dot[:, :, None])).astype(jnp.bfloat16)
        query_sum = query_sum + jnp.einsum(
            "bht,td->bhd", score_grads, key_block, preferred_element_type=jnp.float32
        )
        key_term = (
            jnp.einsum("bht,bhd->td", score_grads, query_heads, preferred_element_type=jnp.float32)
            * score_scale
        )
        value_term = jnp.einsum(
            "bht,bhd->td",
            weights.astype(jnp.bfloat16),
            grad_heads,
            preferred_element_type=jnp.float32,
        )
        return (query_sum, (key_term, value_term))

    zero_query = jnp.zeros(query_heads.shape, jnp.float32)
    query_add, (key_terms, value_terms) = lax.scan(backward_update, zero_query, stacked)
    piece_rows = key_piece.shape[0]
    return (query_add, key_terms.reshape(piece_rows, -1), value_terms.reshape(piece_rows, -1))


def per_device(queries, keys, values, grad_out, lengths, send_order):
    shard_count = lax.axis_size("seq")
    my_index = lax.axis_index("seq")
    tok_rows, head_dim = keys.shape
    group_rows = tok_rows // shard_count
    head_count = queries.shape[1] // head_dim
    score_scale = 1.0 / math.sqrt(head_dim)
    bounds = jnp.cumsum(lengths)
    own_order = lax.dynamic_index_in_dim(send_order, my_index, 0, keepdims=False)
    outgoing = jnp.take(queries, own_order, axis=0)
    picked = lax.all_to_all(outgoing, "seq", split_axis=0, concat_axis=0, tiled=True)
    columns = lax.dynamic_slice_in_dim(send_order, my_index * group_rows, group_rows, 1)
    query_pos = (jnp.arange(shard_count, dtype=jnp.int32)[:, None] * tok_rows + columns).reshape(
        tok_rows
    )
    query_doc = doc_index(query_pos, bounds)
    query_heads = picked.reshape(tok_rows, head_count, head_dim)
    grad_heads = grad_out.reshape(tok_rows, head_count, head_dim)
    context = (query_heads, query_pos, query_doc, bounds, score_scale)
    start_state = (
        jnp.full((tok_rows, head_count), masked_value, jnp.float32),
        jnp.zeros((tok_rows, head_count), jnp.float32),
        jnp.zeros((tok_rows, head_count, head_dim), jnp.float32),
    )
    piece_pair = (
        lax.all_gather(keys, "seq", axis=0, tiled=True),
        lax.all_gather(values, "seq", axis=0, tiled=True),
    )
    run_max, run_total, weighted = forward_piece(start_state, piece_pair[0], piece_pair[1], context)
    attended = weighted / run_total[:, :, None]
    attended_low = attended.astype(jnp.bfloat16)
    log_total = run_max + jnp.log(run_total)
    out_dot = jnp.sum(grad_heads.astype(jnp.float32) * attended_low.astype(jnp.float32), axis=2)
    grad_context = (
        query_heads,
        grad_heads,
        query_pos,
        query_doc,
        bounds,
        score_scale,
        log_total,
        out_dot,
    )
    piece_pair = (
        lax.all_gather(keys, "seq", axis=0, tiled=True),
        lax.all_gather(values, "seq", axis=0, tiled=True),
    )
    query_add, key_part, value_part = backward_piece(piece_pair[0], piece_pair[1], grad_context)
    key_all = key_part
    value_all = value_part
    query_sum, key_all, value_all = (query_add, key_all, value_all)
    key_grad, value_grad = (
        lax.psum_scatter(key_all, "seq", scatter_dimension=0, tiled=True),
        lax.psum_scatter(value_all, "seq", scatter_dimension=0, tiled=True),
    )
    grad_queries = (query_sum * score_scale).reshape(tok_rows, head_count * head_dim)
    return (attended.reshape(tok_rows, head_count * head_dim), grad_queries, key_grad, value_grad)


def solution(mesh):
    placed = (P("seq", "head"), P("seq", "head"), P("seq", "head"), P("seq", "head"), P(), P())
    return jax.shard_map(
        per_device,
        mesh=mesh,
        in_specs=placed,
        out_specs=(P("seq", "head"), P("seq", "head"), P("seq", "head"), P("seq", "head")),
        check_vma=False,
    )
```

profile of v0, /device:TPU:0, one launch (start us, length us, event | category | flops | bytes accessed | tf_op | source)
XLA Modules:
  0.0 306.0 jit_solution(1321556223497053207)
XLA Ops:
  10.8 7.3 %all-to-all-start = ((bf16[8,32,512]{2,1,0:T(8,128)(2,1)}), bf16[8,32,512]{2,1,0:T(8,128)(2,1)S(1)}, u32[]{:S(2)}, u32[]{:S(2)}) async-start(bf16[8,32,512]{2,1,0:T(8,128)(2,1)} %broadcast_select_fusion), calls=%async_computation | async-start | bytes 524288 | tf_op jit(solution)/shard_map/all_to_all | solution.py:116
  22.7 31.9 %all_gather.8 = bf16[2048,128]{1,0:T(8,128)(2,1)S(1)} all-gather(bf16[256,128]{1,0:T(8,128)(2,1)S(1)} %copy-done.13), channel_id=1, replica_groups=mesh['seq'=8,'head'=4] {'seq'}, dimensions={0}, use_global_device_ids=true | all-gather | bytes 589824 | tf_op jit(solution)/shard_map/all_gather | solution.py:131
  54.6 31.2 %all_gather.9 = bf16[2048,128]{1,0:T(8,128)(2,1)S(1)} all-gather(bf16[256,128]{1,0:T(8,128)(2,1)S(1)} %copy-done.14), channel_id=1, replica_groups=mesh['seq'=8,'head'=4] {'seq'}, dimensions={0}, use_global_device_ids=true | all-gather | bytes 589824 | tf_op jit(solution)/shard_map/all_gather | solution.py:132
  86.6 30.8 %while.32 = (s32[]{:T(128)}, f32[256,4]{0,1:T(4,128)S(1)}, f32[256,4]{0,1:T(4,128)S(1)}, f32[256,4,128]{2,0,1:T(8,128)}, s32[256]{0:T(256)S(1)}, /*index=5*/s32[...) while((s32[]{:T(128)}, f32[256,4]{0,1:T(4,128)S(1)}, ...), condition=%wide.wide.region_6.7_spmd.clone, body=%wide.wide.region_2.6_spmd.clone.sunk | while | flops 276067328 | bytes 12661025 | solution.py:66
  86.6 1.2 dynamic_slice.79
  90.1 1.4 fusion.88
  94.3 1.2 dynamic_slice.79
  97.8 1.4 fusion.88
  102.0 1.2 dynamic_slice.79
  105.5 1.4 fusion.88
  113.2 1.4 fusion.88
  119.2 1.8 multiply_reduce_fusion
  121.0 46.2 %while.33 = (s32[]{:T(128)}, f32[256,4,128]{2,0,1:T(8,128)}, f32[4,512,128]{2,1,0:T(8,128)}, f32[4,512,128]{2,1,0:T(8,128)}, s32[256]{0:T(256)S(1)}, /*index=5*/...) while((s32[]{:T(128)}, f32[256,4,128]{2,0,1:T(8,128)}, ...), condition=%wide.wide.region_10.11_spmd.clone, body=%wide.wide.region_8.10_spmd.clone.sunk | while | flops 676028416 | bytes 23222692 | solution.py:101
  121.0 1.2 dynamic_slice.83
  123.9 1.6 fusion.101
  125.6 1.3 fusion.102
  126.9 2.1 fusion.103
  129.0 2.2 convolution_add_fusion.7
  135.3 1.6 fusion.101
  137.0 1.3 fusion.102
  138.3 2.1 fusion.103
  140.4 2.4 convolution_add_fusion.7
  146.9 1.6 fusion.101
  148.6 1.3 fusion.102
  149.9 2.1 fusion.103
  152.0 2.4 convolution_add_fusion.7
  158.5 1.7 fusion.101
  160.2 1.3 fusion.102
  161.5 2.1 fusion.103
  163.6 2.4 convolution_add_fusion.7
  170.2 62.1 %reduce-scatter.3.cloned.1.call-done = f32[256,128]{1,0:T(8,128)} async-done(((f32[2048,128]{1,0:T(8,128)}), f32[256,128]{1,0:T(8,128)}) %reduce-scatter.3.cloned.1.call-update) | async-done | bytes 131088 | tf_op jit(solution)/shard_map/reduce_scatter | solution.py:158
  232.3 66.8 %reduce-scatter.5.cloned.1.call-done = f32[256,128]{1,0:T(8,128)} async-done(((f32[2048,128]{1,0:T(8,128)}), f32[256,128]{1,0:T(8,128)}) %reduce-scatter.5.cloned.1.call-update) | async-done | bytes 131088 | tf_op jit(solution)/shard_map/reduce_scatter | solution.py:159
  (174 shorter events, 49.6 us)
Async XLA Ops:
  7.2 1.6 copy-start
  7.2 10.9 %copy-start.17 = (s32[8,256]{1,0:T(8,128)S(1)}, s32[8,256]{1,0:T(8,128)}, u32[]{:S(2)}) copy-start(s32[8,256]{1,0:T(8,128)} %param.15) | copy-start | bytes 24580
  7.2 12.9 %copy-start.18 = (s32[16]{0:T(128)S(1)}, s32[16]{0:T(128)}, u32[]{:S(2)}) copy-start(s32[16]{0:T(128)} %param.14) | copy-start | bytes 196
  7.2 13.7 %copy-start.12 = (bf16[256,512]{1,0:T(8,128)(2,1)S(1)}, bf16[256,512]{1,0:T(8,128)(2,1)}, u32[]{:S(2)}) copy-start(bf16[256,512]{1,0:T(8,128)(2,1)} %param.13) | copy-start | bytes 786436
  8.8 13.9 %copy-start.13 = (bf16[256,128]{1,0:T(8,128)(2,1)S(1)}, bf16[256,128]{1,0:T(8,128)(2,1)}, u32[]{:S(2)}) copy-start(bf16[256,128]{1,0:T(8,128)(2,1)} %param.11) | copy-start | bytes 196612
  8.8 45.8 %copy-start.14 = (bf16[256,128]{1,0:T(8,128)(2,1)S(1)}, bf16[256,128]{1,0:T(8,128)(2,1)}, u32[]{:S(2)}) copy-start(bf16[256,128]{1,0:T(8,128)(2,1)} %param.12) | copy-start | bytes 196612
  10.8 75.0 %all-to-all-start = ((bf16[8,32,512]{2,1,0:T(8,128)(2,1)}), bf16[8,32,512]{2,1,0:T(8,128)(2,1)S(1)}, u32[]{:S(2)}, u32[]{:S(2)}) async-start(bf16[8,32,512]{2,1,0:T(8,128)(2,1)} %broadcast_select_fusion), calls=%async_computation | async-start | bytes 524288 | tf_op jit(solution)/shard_map/all_to_all | solution.py:116
  18.1 214.2 %reduce-scatter.3.cloned.1.call-start = ((), (), s32[]{:S(2)}) async-start(), calls=%async_computation.3 | async-start | bytes 1179648 | tf_op jit(solution)/shard_map/reduce_scatter | solution.py:158
  18.2 68.4 %copy-start.15 = (s32[8,32]{1,0:T(8,128)}, s32[8,32]{1,0:T(8,128)S(1)}, u32[]{:S(2)}) copy-start(s32[8,32]{1,0:T(8,128)S(1)} %dynamic-slice_add_fusion) | copy-start | bytes 3076
  21.1 65.5 %copy-start.8 = (bf16[256,512]{0,1:T(8,128)(2,1)}, bf16[256,512]{0,1:T(8,128)(2,1)S(1)}, u32[]{:S(2)}) copy-start(bf16[256,512]{0,1:T(8,128)(2,1)S(1)} %copy.30) | copy-start | bytes 786436
  117.3 3.7 %copy-start.16 = (s32[256]{0:T(256)S(1)}, s32[256]{0:T(256)}, u32[]{:S(2)}) copy-start(s32[256]{0:T(256)} %le.73) | copy-start | bytes 3076
  121.0 4.5 %copy-start.4 = (bf16[4,512,128]{2,1,0:T(8,128)(2,1)}, bf16[4,512,128]{2,1,0:T(8,128)(2,1)S(1)}, u32[]{:S(2)}) copy-start(bf16[4,512,128]{2,1,0:T(8,128)(2,1)S(1)} %get-tuple-element.698) | copy-start | bytes 1572868 | tf_op jit(solution)/shard_map/while
  121.0 4.5 %copy-start.6 = (bf16[4,512,128]{2,1,0:T(8,128)(2,1)}, bf16[4,512,128]{2,1,0:T(8,128)(2,1)S(1)}, u32[]{:S(2)}) copy-start(bf16[4,512,128]{2,1,0:T(8,128)(2,1)S(1)} %get-tuple-element.701) | copy-start | bytes 1572868 | tf_op jit(solution)/shard_map/while
  121.0 4.5 %copy-start.1 = (bf16[256,4,128]{2,0,1:T(8,128)(2,1)S(1)}, bf16[256,4,128]{2,0,1:T(8,128)(2,1)}, u32[]{:S(2)}) copy-start(bf16[256,4,128]{2,0,1:T(8,128)(2,1)} %get-tuple-element.702) | copy-start | bytes 786436 | tf_op jit(solution)/shard_map/while
  129.0 2.2 copy-start.2
  131.2 1.2 copy-start.7
  132.4 4.5 %copy-start.4 = (bf16[4,512,128]{2,1,0:T(8,128)(2,1)}, bf16[4,512,128]{2,1,0:T(8,128)(2,1)S(1)}, u32[]{:S(2)}) copy-start(bf16[4,512,128]{2,1,0:T(8,128)(2,1)S(1)} %get-tuple-element.698) | copy-start | bytes 1572868 | tf_op jit(solution)/shard_map/while
  132.4 4.5 %copy-start.6 = (bf16[4,512,128]{2,1,0:T(8,128)(2,1)}, bf16[4,512,128]{2,1,0:T(8,128)(2,1)S(1)}, u32[]{:S(2)}) copy-start(bf16[4,512,128]{2,1,0:T(8,128)(2,1)S(1)} %get-tuple-element.701) | copy-start | bytes 1572868 | tf_op jit(solution)/shard_map/while
  132.4 4.5 %copy-start.1 = (bf16[256,4,128]{2,0,1:T(8,128)(2,1)S(1)}, bf16[256,4,128]{2,0,1:T(8,128)(2,1)}, u32[]{:S(2)}) copy-start(bf16[256,4,128]{2,0,1:T(8,128)(2,1)} %get-tuple-element.702) | copy-start | bytes 786436 | tf_op jit(solution)/shard_map/while
  140.4 2.4 copy-start.2
  144.0 4.5 %copy-start.4 = (bf16[4,512,128]{2,1,0:T(8,128)(2,1)}, bf16[4,512,128]{2,1,0:T(8,128)(2,1)S(1)}, u32[]{:S(2)}) copy-start(bf16[4,512,128]{2,1,0:T(8,128)(2,1)S(1)} %get-tuple-element.698) | copy-start | bytes 1572868 | tf_op jit(solution)/shard_map/while
  144.0 4.5 %copy-start.6 = (bf16[4,512,128]{2,1,0:T(8,128)(2,1)}, bf16[4,512,128]{2,1,0:T(8,128)(2,1)S(1)}, u32[]{:S(2)}) copy-start(bf16[4,512,128]{2,1,0:T(8,128)(2,1)S(1)} %get-tuple-element.701) | copy-start | bytes 1572868 | tf_op jit(solution)/shard_map/while
  144.0 4.5 %copy-start.1 = (bf16[256,4,128]{2,0,1:T(8,128)(2,1)S(1)}, bf16[256,4,128]{2,0,1:T(8,128)(2,1)}, u32[]{:S(2)}) copy-start(bf16[256,4,128]{2,0,1:T(8,128)(2,1)} %get-tuple-element.702) | copy-start | bytes 786436 | tf_op jit(solution)/shard_map/while
  152.0 2.4 copy-start.2
  154.4 1.2 copy-start.7
  155.6 4.5 %copy-start.4 = (bf16[4,512,128]{2,1,0:T(8,128)(2,1)}, bf16[4,512,128]{2,1,0:T(8,128)(2,1)S(1)}, u32[]{:S(2)}) copy-start(bf16[4,512,128]{2,1,0:T(8,128)(2,1)S(1)} %get-tuple-element.698) | copy-start | bytes 1572868 | tf_op jit(solution)/shard_map/while
  155.6 4.5 %copy-start.6 = (bf16[4,512,128]{2,1,0:T(8,128)(2,1)}, bf16[4,512,128]{2,1,0:T(8,128)(2,1)S(1)}, u32[]{:S(2)}) copy-start(bf16[4,512,128]{2,1,0:T(8,128)(2,1)S(1)} %get-tuple-element.701) | copy-start | bytes 1572868 | tf_op jit(solution)/shard_map/while
  155.6 4.5 %copy-start.1 = (bf16[256,4,128]{2,0,1:T(8,128)(2,1)S(1)}, bf16[256,4,128]{2,0,1:T(8,128)(2,1)}, u32[]{:S(2)}) copy-start(bf16[256,4,128]{2,0,1:T(8,128)(2,1)} %get-tuple-element.702) | copy-start | bytes 786436 | tf_op jit(solution)/shard_map/while
  163.6 2.4 copy-start.2
  166.1 1.2 copy-start.7
  167.3 2.0 copy-start.3
  167.3 131.8 %reduce-scatter.5.cloned.1.call-start = ((), (), s32[]{:S(2)}) async-start(), calls=%async_computation.4 | async-start | bytes 1179648 | tf_op jit(solution)/shard_map/reduce_scatter | solution.py:159
  (14 other events, 14.2 us)
Sparse Core Ops, SparseCore 0:
  167.4 64.8 reduce-scatter.2
  236.6 62.4 reduce-scatter.4
where the time goes:
time: 307 us; the launch traced here: 306 us
  waiting for transfers between devices  130 us (42%)
  blocking collectives  63 us (21%)
  matrix products  43.7 us (14%)
  other arithmetic  24.7 us (8%)
  local copies, waits for them, and re-layouts  22.9 us (7%)
  between operations  14.2 us (5%)
  starting transfers between devices  7.36 us (2%)
    reduce_scatter x1, waiting for transfers between devices, per_device(): lax.psum_scatter(value_all, 'seq', scatter_dimension=0, tiled=True)  66.8 us
    reduce_scatter x1, waiting for transfers between devices, per_device(): lax.psum_scatter(key_all, 'seq', scatter_dimension=0, tiled=True)  62.1 us
    all_gather x1, blocking collectives, per_device(): lax.all_gather(keys, 'seq', axis=0, tiled=True)  31.9 us
    all_gather x1, blocking collectives, per_device(): lax.all_gather(values, 'seq', axis=0, tiled=True)  31.2 us
    dot_general x8, matrix products, block_scores(): jnp.einsum('bhd,td->bht', query_heads, key_block, preferred_element_type=...  12.3 us
    dynamic_slice x8, local copies, waits for them, and re-layouts, forward_piece(): run_state, _ = lax.scan(forward_update, run_state, stacked)  9.91 us
    dot_general x4, matrix products, backward_update(): jnp.einsum('bht,td->bhd', score_grads, key_block, preferred_element_type=...  9.48 us
    dot_general x4, matrix products, backward_update(): jnp.einsum('bht,bhd->td', score_grads, query_heads, preferred_element_typ...  8.38 us
  transfers between devices with their start and end apart: 3, of which 2 were waited for; matrix products, arithmetic and copies ran while one was open for 2% of the time, Pallas kernels for 0%

commit v1 on v0

v1 whole, which is shorter than its diff:
```python
import functools
import math

import jax
import jax.numpy as jnp
from jax import lax
from jax.experimental import pallas as pl
from jax.experimental.pallas import tpu as pltpu
from jax.sharding import PartitionSpec as P

MESH = pl.DeviceIdType.MESH
masked_value = -1e30


def dot_nt(a, b):
    return lax.dot_general(a, b, (((1,), (1,)), ((), ())), preferred_element_type=jnp.float32)


def dot_nn(a, b):
    return jnp.dot(a, b, preferred_element_type=jnp.float32)


def kernel(
    n,
    back,
    q_ref,
    k_ref,
    v_ref,
    g_ref,
    len_ref,
    order_ref,
    att_ref,
    gq_ref,
    gk_ref,
    gv_ref,
    kwin,
    vwin,
    gbuf,
    att_buf,
    gq_buf,
    bias,
    weights,
    gk_send,
    gv_send,
    gk_land,
    gv_land,
    kv_ssem,
    kv_rsem,
    g_ssem,
    g_rsem,
    a_ssem,
    a_rsem,
    gq_ssem,
    gq_rsem,
    gkv_ssem,
    gkv_rsem,
    own_sem,
):
    me = lax.axis_index("seq")
    tok, head_dim = k_ref.shape
    group = tok // n
    heads = q_ref.shape[1] // head_dim
    window = (back + 1) * tok
    scale = 1.0 / math.sqrt(head_dim)

    def peer(offset):
        return lax.rem(me + offset, n)

    def remote(src, dst, ssem, rsem, target):
        return pltpu.make_async_remote_copy(
            src_ref=src,
            dst_ref=dst,
            send_sem=ssem,
            recv_sem=rsem,
            device_id={"seq": target},
            device_id_type=MESH,
        )

    def halo_in(b):
        rows = pl.ds((back - b) * tok, tok)
        target = peer(b)
        return (
            remote(k_ref, kwin.at[rows], kv_ssem.at[0, b - 1], kv_rsem.at[0, b - 1], target),
            remote(v_ref, vwin.at[rows], kv_ssem.at[1, b - 1], kv_rsem.at[1, b - 1], target),
        )

    def halo_out(b):
        target = peer(n - b)
        return (
            remote(
                gk_send.at[b - 1],
                gk_land.at[b - 1],
                gkv_ssem.at[0, b - 1],
                gkv_rsem.at[0, b - 1],
                target,
            ),
            remote(
                gv_send.at[b - 1],
                gv_land.at[b - 1],
                gkv_ssem.at[1, b - 1],
                gkv_rsem.at[1, b - 1],
                target,
            ),
        )

    def spread(src, dst, ssem, rsem, offset):
        target = peer(offset)
        return remote(src.at[target], dst.at[me], ssem.at[offset], rsem.at[offset], target)

    barrier = pltpu.get_barrier_semaphore()
    for offset in range(1, n):
        pl.semaphore_signal(
            barrier, inc=1, device_id={"seq": peer(offset)}, device_id_type=MESH
        )

    own_grad = pltpu.make_async_copy(g_ref.at[me], gbuf.at[me], own_sem.at[0])
    own_grad.start()
    kwin[back * tok :, :] = k_ref[...]
    vwin[back * tok :, :] = v_ref[...]
    for b in range(1, back + 1):

        @pl.when(me < b)
        def _():
            kwin[(back - b) * tok : (back - b + 1) * tok, :] = jnp.zeros((tok, head_dim), kwin.dtype)
            vwin[(back - b) * tok : (back - b + 1) * tok, :] = jnp.zeros((tok, head_dim), vwin.dtype)

    pl.semaphore_wait(barrier, n - 1)
    for b in range(1, back + 1):

        @pl.when(me + b < n)
        def _():
            for copy in halo_in(b):
                copy.start()

    for offset in range(1, n):
        spread(g_ref, gbuf, g_ssem, g_rsem, offset).start()

    order = order_ref[pl.ds(me, 1), :]
    one_hot = (lax.broadcasted_iota(jnp.int32, (tok, tok), 0) == order).astype(jnp.float32)
    picked = dot_nn(one_hot.T.astype(jnp.bfloat16), q_ref[...]).astype(jnp.bfloat16)
    query_pos = order + me * tok
    start = jnp.zeros_like(query_pos)
    bound = jnp.int32(0)
    for d in range(len_ref.shape[0]):
        bound = bound + len_ref[d]
        start = jnp.where(query_pos >= bound, bound, start)
    key_pos = lax.broadcasted_iota(jnp.int32, (window, tok), 0) + (me - back) * tok
    allowed = (key_pos >= start) & (key_pos <= query_pos)
    bias[...] = jnp.where(allowed, 0.0, masked_value)

    for b in range(1, back + 1):

        @pl.when(me >= b)
        def _():
            for copy in halo_in(b):
                copy.wait_recv()

    key_all = kwin[...]
    value_all = vwin[...]
    key_t = key_all.astype(jnp.float32).T.astype(jnp.bfloat16)
    value_t = value_all.astype(jnp.float32).T.astype(jnp.bfloat16)
    exponent = scale * math.log2(math.e)

    att_cols = []
    for h in range(heads):
        cols = slice(h * head_dim, (h + 1) * head_dim)
        scores = dot_nt(key_all, picked[:, cols]) + bias[...]
        row_max = jnp.max(scores, axis=0, keepdims=True)
        exps = jnp.exp2((scores - row_max) * exponent)
        weight = exps * (1.0 / jnp.sum(exps, axis=0, keepdims=True))
        weights[h] = weight
        att_t = dot_nn(value_t, weight.astype(jnp.bfloat16))
        att_low = att_t.T
        att_cols.append(att_t.astype(jnp.bfloat16).astype(jnp.float32))
        att_buf[:, :, cols] = att_low.reshape(n, group, head_dim).astype(jnp.bfloat16)
    own_att = pltpu.make_async_copy(att_buf.at[me], att_ref.at[me], own_sem.at[1])
    own_att.start()
    for offset in range(1, n):
        spread(att_buf, att_ref, a_ssem, a_rsem, offset).start()

    own_grad.wait()
    for offset in range(1, n):
        spread(g_ref, gbuf, g_ssem, g_rsem, offset).wait_recv()

    key_sum = None
    for h in range(heads):
        cols = slice(h * head_dim, (h + 1) * head_dim)
        grad_float = gbuf[:, :, cols].astype(jnp.float32).reshape(tok, head_dim)
        grad = grad_float.astype(jnp.bfloat16)
        out_dot = jnp.sum(grad_float.T * att_cols[h], axis=0, keepdims=True)
        weight = weights[h]
        score_grads = (weight * (dot_nt(value_all, grad) - out_dot)).astype(jnp.bfloat16)
        query_grad = (dot_nn(key_t, score_grads) * scale).T
        gq_buf[:, :, cols] = query_grad.reshape(n, group, head_dim).astype(jnp.bfloat16)
        key_term = dot_nn(score_grads, picked[:, cols])
        value_term = dot_nn(weight.astype(jnp.bfloat16), grad)
        key_sum = key_term if key_sum is None else key_sum + key_term
        value_sum = value_term if h == 0 else value_sum + value_term

    own_gq = pltpu.make_async_copy(gq_buf.at[me], gq_ref.at[me], own_sem.at[2])
    own_gq.start()
    for offset in range(1, n):
        spread(gq_buf, gq_ref, gq_ssem, gq_rsem, offset).start()
    key_sum = key_sum * scale
    for b in range(1, back + 1):
        rows = slice((back - b) * tok, (back - b + 1) * tok)
        gk_send[b - 1] = key_sum[rows, :].astype(jnp.bfloat16)
        gv_send[b - 1] = value_sum[rows, :].astype(jnp.bfloat16)

        @pl.when(me >= b)
        def _():
            for copy in halo_out(b):
                copy.start()

    gk_ref[...] = key_sum[back * tok :, :]
    gv_ref[...] = value_sum[back * tok :, :]
    for b in range(1, back + 1):

        @pl.when(me + b < n)
        def _():
            for copy in halo_in(b):
                copy.wait_send()
            for copy in halo_out(b):
                copy.wait_recv()
            gk_ref[...] += gk_land[b - 1].astype(jnp.float32)
            gv_ref[...] += gv_land[b - 1].astype(jnp.float32)

        @pl.when(me >= b)
        def _():
            for copy in halo_out(b):
                copy.wait_send()

    own_att.wait()
    own_gq.wait()
    for offset in range(1, n):
        spread(g_ref, gbuf, g_ssem, g_rsem, offset).wait_send()
        spread(att_buf, att_ref, a_ssem, a_rsem, offset).wait()
        spread(gq_buf, gq_ref, gq_ssem, gq_rsem, offset).wait()


def per_device(n, queries, keys, values, grad_out, lengths, send_order):
    tok, head_dim = keys.shape
    width = queries.shape[1]
    heads = width // head_dim
    group = tok // n
    longest = n * tok // 4
    back = min(n - 1, -(-(longest - 1) // tok))
    window = (back + 1) * tok
    flops = 2 * tok * heads * window * head_dim * 5
    vmem = pl.BlockSpec(memory_space=pltpu.VMEM)
    hbm = pl.BlockSpec(memory_space=pl.ANY)
    smem = pl.BlockSpec(memory_space=pltpu.SMEM)
    dma = pltpu.SemaphoreType.DMA
    att, gq, gk, gv = pl.pallas_call(
        functools.partial(kernel, n, back),
        out_shape=(
            jax.ShapeDtypeStruct((n, group, width), jnp.bfloat16),
            jax.ShapeDtypeStruct((n, group, width), jnp.bfloat16),
            jax.ShapeDtypeStruct((tok, head_dim), jnp.float32),
            jax.ShapeDtypeStruct((tok, head_dim), jnp.float32),
        ),
        in_specs=[vmem, vmem, vmem, hbm, smem, vmem],
        out_specs=(hbm, hbm, vmem, vmem),
        scratch_shapes=[
            pltpu.VMEM((window, head_dim), jnp.bfloat16),
            pltpu.VMEM((window, head_dim), jnp.bfloat16),
            pltpu.VMEM((n, group, width), jnp.bfloat16),
            pltpu.VMEM((n, group, width), jnp.bfloat16),
            pltpu.VMEM((n, group, width), jnp.bfloat16),
            pltpu.VMEM((window, tok), jnp.float32),
            pltpu.VMEM((heads, window, tok), jnp.float32),
            pltpu.VMEM((back, tok, head_dim), jnp.bfloat16),
            pltpu.VMEM((back, tok, head_dim), jnp.bfloat16),
            pltpu.VMEM((back, tok, head_dim), jnp.bfloat16),
            pltpu.VMEM((back, tok, head_dim), jnp.bfloat16),
            dma((2, back)),
            dma((2, back)),
            dma((n,)),
            dma((n,)),
            dma((n,)),
            dma((n,)),
            dma((n,)),
            dma((n,)),
            dma((2, back)),
            dma((2, back)),
            dma((3,)),
        ],
        compiler_params=pltpu.CompilerParams(
            collective_id=0, has_side_effects=True, vmem_limit_bytes=48 * 1024 * 1024
        ),
        cost_estimate=pl.CostEstimate(
            flops=flops, bytes_accessed=6 * tok * width, transcendentals=tok * heads * window
        ),
    )(queries, keys, values, grad_out.reshape(n, group, width), lengths, send_order)
    return (
        att.reshape(tok, width).astype(jnp.float32),
        gq.reshape(tok, width).astype(jnp.float32),
        gk,
        gv,
    )


def solution(mesh):
    placed = (P("seq", "head"), P("seq", "head"), P("seq", "head"), P("seq", "head"), P(), P())
    return jax.shard_map(
        functools.partial(per_device, mesh.shape["seq"]),
        mesh=mesh,
        in_specs=placed,
        out_specs=(P("seq", "head"), P("seq", "head"), P("seq", "head"), P("seq", "head")),
        check_vma=False,
    )
```

time: 307 us -> 38.4 us (0.13)
  waiting for transfers between devices: 130 us -> 0 us
  blocking collectives: 63 us -> 0 us
  matrix products: 43.7 us -> 0 us
  Pallas kernels: 0 us -> 30.1 us
  other arithmetic: 24.7 us -> 1.13 us
  local copies, waits for them, and re-layouts: 22.9 us -> 6.23 us
  between operations: 14.2 us -> 0.66 us
  starting transfers between devices: 7.36 us -> 0 us
    reduce_scatter x2 -> x0, waiting for transfers between devices: 129 us -> none  [the longest x1 66.8 us: per_device(): lax.psum_scatter(value_all, 'seq', scatter_dimension=0, tiled=True)]
    all_gather x2 -> x0, blocking collectives: 63 us -> none  [the longest x1 31.9 us: per_device(): lax.all_gather(keys, 'seq', axis=0, tiled=True)]
    dot_general x28 -> x0, matrix products: 43.7 us -> none  [the longest x8 12.3 us: block_scores(): jnp.einsum('bhd,td->bht', query_heads, key_block, preferred_element_type=...]
    pallas_call x0 -> x1, Pallas kernels: none -> 30.1 us  [per_device(): pl.pallas_call(functools.partial(kernel, n, back), out_shape=(jax.ShapeDt...]
    reduce_sum x14 -> x0, other arithmetic: 10.9 us -> none  [the longest x9 6.92 us: doc_index(): jnp.sum((positions[:, None] >= bounds[None, :]).astype(jnp.int32), axis=1)]
    dynamic_slice x9 -> x0, local copies, waits for them, and re-layouts: 10.6 us -> none  [the longest x8 9.91 us: forward_piece(): run_state, _ = lax.scan(forward_update, run_state, stacked)]
    all_to_all x1 -> x0, starting transfers between devices: 7.28 us -> none  [per_device(): lax.all_to_all(outgoing, 'seq', split_axis=0, concat_axis=0, tiled=True)]
    while x69 -> x0, local copies, waits for them, and re-layouts: 6.51 us -> none
  transfers between devices with their start and end apart: 3 -> 0, of which waited for: 2 -> 0; matrix products, arithmetic and copies ran while one was open for 2% -> 0% of each run, Pallas kernels for 0% -> 0%
where the time goes in v1:
time: 38.4 us; the launch traced here: 38.1 us
  Pallas kernels  30.1 us (78%)
  local copies, waits for them, and re-layouts  6.23 us (16%)
  other arithmetic  1.13 us (3%)
  between operations  0.66 us (2%)
    pallas_call x1, Pallas kernels, per_device(): pl.pallas_call(functools.partial(kernel, n, back), out_shape=(jax.ShapeDt...  30.1 us
    unnamed x14, local copies, waits for them, and re-layouts  6.23 us
    convert_element_type x1, other arithmetic, per_device(): gq.reshape(tok, width).astype(jnp.float32)  1.13 us

profile of v1, /device:TPU:0, one launch (start us, length us, event | category | flops | bytes accessed | tf_op | source)
XLA Modules:
  0.0 38.1 jit_solution(168421543019753920)
XLA Ops:
  0.6 0.0 copy-start.5
  0.6 0.6 %copy-done.5 = s32[16]{0:T(128)S(1)} copy-done((s32[16]{0:T(128)S(1)}, s32[16]{0:T(128)}, u32[]{:S(2)}) %copy-start.5) | copy-done | bytes 88
  1.3 0.0 copy-start
  1.3 0.9 %copy-done = bf16[256,512]{1,0:T(8,128)(2,1)S(1)} copy-done((bf16[256,512]{1,0:T(8,128)(2,1)S(1)}, bf16[256,512]{1,0:T(8,128)(2,1)}, u32[]{:S(2)}) %copy-start) | copy-done | bytes 262168
  2.2 0.0 copy-start.1
  2.2 0.9 %copy-done.1 = bf16[256,512]{1,0:T(8,128)(2,1)S(1)} copy-done((bf16[256,512]{1,0:T(8,128)(2,1)S(1)}, bf16[256,512]{1,0:T(8,128)(2,1)}, u32[]{:S(2)}) %copy-start.1) | copy-done | bytes 262168
  3.2 0.0 copy-start.2
  3.2 0.8 %copy-done.2 = bf16[256,128]{1,0:T(8,128)(2,1)S(1)} copy-done((bf16[256,128]{1,0:T(8,128)(2,1)S(1)}, bf16[256,128]{1,0:T(8,128)(2,1)}, u32[]{:S(2)}) %copy-start.2) | copy-done | bytes 65560
  4.0 0.0 copy-start.3
  4.0 0.8 %copy-done.3 = bf16[256,128]{1,0:T(8,128)(2,1)S(1)} copy-done((bf16[256,128]{1,0:T(8,128)(2,1)S(1)}, bf16[256,128]{1,0:T(8,128)(2,1)}, u32[]{:S(2)}) %copy-start.3) | copy-done | bytes 65560
  4.9 0.0 copy-start.4
  4.9 0.7 %copy-done.4 = s32[8,256]{1,0:T(8,128)S(1)} copy-done((s32[8,256]{1,0:T(8,128)S(1)}, s32[8,256]{1,0:T(8,128)}, u32[]{:S(2)}) %copy-start.4) | copy-done | bytes 8216
  5.6 30.1 %shard_map.93 = (bf16[8,32,512]{2,1,0:T(8,128)(2,1)S(1)}, bf16[8,32,512]{2,1,0:T(8,128)(2,1)S(1)}, f32[256,128]{1,0:T(8,128)S(1)}, f32[256,128]{1,0:T(8,128)S(1)}) custom-call(bf16[256,512]{1,0:T(8,128)(2,1)S(1)} %copy-done, bf16[256,128]{1,0:T(8,128)(2,1)S(1)} %copy-done.2, bf16[256,128]{1,0:T(8,128)(2,1)S(1)} %copy-done.3, ...), custom_call_target="tpu_custom_call" | custom-call | flops 1006632960 | bytes 786432 | tf_op jit(solution)/shard_map/pallas_call | solution.py:254
  35.7 1.1 %bitcast_convert_fusion = (f32[256,512]{1,0:T(8,128)}, f32[256,512]{1,0:T(8,128)}) fusion(bf16[8,32,512]{2,1,0:T(8,128)(2,1)S(1)} %get-tuple-element.9, bf16[8,32,512]{2,1,0:T(8,128)(2,1)S(1)} %get-tuple-element.8), kind=kLoop, calls=%fused_computation | loop fusion | flops 262144 | bytes 1572864 | tf_op jit(solution)/shard_map/convert_element_type | solution.py:297
  36.8 0.7 %copy.12 = f32[256,128]{1,0:T(8,128)} copy(f32[256,128]{1,0:T(8,128)S(1)} %get-tuple-element.20) | data formatting | bytes 262144
  37.4 0.7 %copy.13 = f32[256,128]{1,0:T(8,128)} copy(f32[256,128]{1,0:T(8,128)S(1)} %get-tuple-element.21) | data formatting | bytes 262144
Async XLA Ops:
  0.6 0.7 %copy-start.5 = (s32[16]{0:T(128)S(1)}, s32[16]{0:T(128)}, u32[]{:S(2)}) copy-start(s32[16]{0:T(128)} %len_ref.1) | copy-start | bytes 196
  1.3 0.9 %copy-start = (bf16[256,512]{1,0:T(8,128)(2,1)S(1)}, bf16[256,512]{1,0:T(8,128)(2,1)}, u32[]{:S(2)}) copy-start(bf16[256,512]{1,0:T(8,128)(2,1)} %q_ref.1) | copy-start | bytes 786436
  2.2 0.9 %copy-start.1 = (bf16[256,512]{1,0:T(8,128)(2,1)S(1)}, bf16[256,512]{1,0:T(8,128)(2,1)}, u32[]{:S(2)}) copy-start(bf16[256,512]{1,0:T(8,128)(2,1)} %param.9) | copy-start | bytes 786436
  3.2 0.8 %copy-start.2 = (bf16[256,128]{1,0:T(8,128)(2,1)S(1)}, bf16[256,128]{1,0:T(8,128)(2,1)}, u32[]{:S(2)}) copy-start(bf16[256,128]{1,0:T(8,128)(2,1)} %k_ref.1) | copy-start | bytes 196612
  4.0 0.8 %copy-start.3 = (bf16[256,128]{1,0:T(8,128)(2,1)S(1)}, bf16[256,128]{1,0:T(8,128)(2,1)}, u32[]{:S(2)}) copy-start(bf16[256,128]{1,0:T(8,128)(2,1)} %v_ref.1) | copy-start | bytes 196612
  4.9 0.7 %copy-start.4 = (s32[8,256]{1,0:T(8,128)S(1)}, s32[8,256]{1,0:T(8,128)}, u32[]{:S(2)}) copy-start(s32[8,256]{1,0:T(8,128)} %order_ref.1) | copy-start | bytes 24580

commit v2 on v1

--- a/solution.py
+++ b/solution.py
@@ -23,16 +23,19 @@
 def kernel(
     n,
     back,
-    q_ref,
+    q_hbm,
     k_ref,
     v_ref,
     g_ref,
-    len_ref,
-    order_ref,
+    len_hbm,
+    order_hbm,
     att_ref,
     gq_ref,
     gk_ref,
     gv_ref,
+    q_ref,
+    len_ref,
+    order_ref,
     kwin,
     vwin,
     gbuf,
@@ -59,6 +62,7 @@
     me = lax.axis_index("seq")
     tok, head_dim = k_ref.shape
     group = tok // n
+    parts = a_ssem.shape[0]
     heads = q_ref.shape[1] // head_dim
     window = (back + 1) * tok
     scale = 1.0 / math.sqrt(head_dim)
@@ -107,16 +111,35 @@
         target = peer(offset)
         return remote(src.at[target], dst.at[me], ssem.at[offset], rsem.at[offset], target)
 
+    def spread_part(src, dst, ssem, rsem, part, offset):
+        target = peer(offset)
+        width = heads // parts * head_dim
+        cols = pl.ds(part * width, width)
+        return remote(
+            src.at[target, :, cols],
+            dst.at[me, :, cols],
+            ssem.at[part, offset],
+            rsem.at[part, offset],
+            target,
+        )
+
     barrier = pltpu.get_barrier_semaphore()
     for offset in range(1, n):
         pl.semaphore_signal(
             barrier, inc=1, device_id={"seq": peer(offset)}, device_id_type=MESH
         )
 
-    own_grad = pltpu.make_async_copy(g_ref.at[me], gbuf.at[me], own_sem.at[0])
-    own_grad.start()
-    kwin[back * tok :, :] = k_ref[...]
-    vwin[back * tok :, :] = v_ref[...]
+    own_rows = pl.ds(back * tok, tok)
+    local = [
+        pltpu.make_async_copy(order_hbm, order_ref, own_sem.at[0]),
+        pltpu.make_async_copy(len_hbm, len_ref, own_sem.at[1]),
+        pltpu.make_async_copy(q_hbm, q_ref, own_sem.at[2]),
+        pltpu.make_async_copy(k_ref, kwin.at[own_rows], own_sem.at[3]),
+        pltpu.make_async_copy(v_ref, vwin.at[own_rows], own_sem.at[4]),
+        pltpu.make_async_copy(g_ref.at[me], gbuf.at[me], own_sem.at[5]),
+    ]
+    for copy in local:
+        copy.start()
     for b in range(1, back + 1):
 
         @pl.when(me < b)
@@ -133,7 +156,13 @@
                 copy.start()
 
     for offset in range(1, n):
-        spread(g_ref, gbuf, g_ssem, g_rsem, offset).start()
+
+        @pl.when(peer(offset) < me)
+        def _():
+            spread(g_ref, gbuf, g_ssem, g_rsem, offset).start()
+
+    for copy in local:
+        copy.wait()
 
     order = order_ref[pl.ds(me, 1), :]
     one_hot = (lax.broadcasted_iota(jnp.int32, (tok, tok), 0) == order).astype(jnp.float32)
@@ -150,6 +179,19 @@
 
     for b in range(1, back + 1):
 
+        @pl.when(me + b < n)
+        def _():
+            for copy in halo_in(b):
+                copy.wait_send()
+
+    for offset in range(1, n):
+
+        @pl.when(peer(offset) > me)
+        def _():
+            spread(g_ref, gbuf, g_ssem, g_rsem, offset).start()
+
+    for b in range(1, back + 1):
+
         @pl.when(me >= b)
         def _():
             for copy in halo_in(b):
@@ -173,12 +215,13 @@
         att_low = att_t.T
         att_cols.append(att_t.astype(jnp.bfloat16).astype(jnp.float32))
         att_buf[:, :, cols] = att_low.reshape(n, group, head_dim).astype(jnp.bfloat16)
-    own_att = pltpu.make_async_copy(att_buf.at[me], att_ref.at[me], own_sem.at[1])
+        part = (h + 1) * parts // heads - 1
+        if (h + 1) * parts % heads == 0:
+            for offset in range(1, n):
+                spread_part(att_buf, att_ref, a_ssem, a_rsem, part, offset).start()
+    own_att = pltpu.make_async_copy(att_buf.at[me], att_ref.at[me], own_sem.at[6])
     own_att.start()
-    for offset in range(1, n):
-        spread(att_buf, att_ref, a_ssem, a_rsem, offset).start()
-
-    own_grad.wait()
+
     for offset in range(1, n):
         spread(g_ref, gbuf, g_ssem, g_rsem, offset).wait_recv()
 
@@ -192,15 +235,15 @@
         score_grads = (weight * (dot_nt(value_all, grad) - out_dot)).astype(jnp.bfloat16)
         query_grad = (dot_nn(key_t, score_grads) * scale).T
         gq_buf[:, :, cols] = query_grad.reshape(n, group, head_dim).astype(jnp.bfloat16)
+        part = (h + 1) * parts // heads - 1
+        if (h + 1) * parts % heads == 0:
+            for offset in range(1, n):
+                spread_part(gq_buf, gq_ref, gq_ssem, gq_rsem, part, offset).start()
         key_term = dot_nn(score_grads, picked[:, cols])
         value_term = dot_nn(weight.astype(jnp.bfloat16), grad)
         key_sum = key_term if key_sum is None else key_sum + key_term
         value_sum = value_term if h == 0 else value_sum + value_term
 
-    own_gq = pltpu.make_async_copy(gq_buf.at[me], gq_ref.at[me], own_sem.at[2])
-    own_gq.start()
-    for offset in range(1, n):
-        spread(gq_buf, gq_ref, gq_ssem, gq_rsem, offset).start()
     key_sum = key_sum * scale
     for b in range(1, back + 1):
         rows = slice((back - b) * tok, (back - b + 1) * tok)
@@ -212,14 +255,14 @@
             for copy in halo_out(b):
                 copy.start()
 
+    own_gq = pltpu.make_async_copy(gq_buf.at[me], gq_ref.at[me], own_sem.at[7])
+    own_gq.start()
     gk_ref[...] = key_sum[back * tok :, :]
     gv_ref[...] = value_sum[back * tok :, :]
     for b in range(1, back + 1):
 
         @pl.when(me + b < n)
         def _():
-            for copy in halo_in(b):
-                copy.wait_send()
             for copy in halo_out(b):
                 copy.wait_recv()
             gk_ref[...] += gk_land[b - 1].astype(jnp.float32)
@@ -234,8 +277,16 @@
     own_gq.wait()
     for offset in range(1, n):
         spread(g_ref, gbuf, g_ssem, g_rsem, offset).wait_send()
-        spread(att_buf, att_ref, a_ssem, a_rsem, offset).wait()
-        spread(gq_buf, gq_ref, gq_ssem, gq_rsem, offset).wait()
+        for part in range(parts):
+            spread_part(att_buf, att_ref, a_ssem, a_rsem, part, offset).wait()
+            spread_part(gq_buf, gq_ref, gq_ssem, gq_rsem, part, offset).wait()
+
+
+def widen(att_ref, gq_ref, gk_ref, gv_ref, att_out, gq_out, gk_out, gv_out):
+    att_out[...] = att_ref[...].astype(jnp.float32)
+    gq_out[...] = gq_ref[...].astype(jnp.float32)
+    gk_out[...] = gk_ref[...]
+    gv_out[...] = gv_ref[...]
 
 
 def per_device(n, queries, keys, values, grad_out, lengths, send_order):
@@ -248,8 +299,9 @@
     window = (back + 1) * tok
     flops = 2 * tok * heads * window * head_dim * 5
     vmem = pl.BlockSpec(memory_space=pltpu.VMEM)
-    hbm = pl.BlockSpec(memory_space=pl.ANY)
-    smem = pl.BlockSpec(memory_space=pltpu.SMEM)
+    hbm = pl.BlockSpec(memory_space=pltpu.HBM)
+    parts = math.gcd(heads, 2)
+    vmem_limit = 62 * 1024 * 1024
     dma = pltpu.SemaphoreType.DMA
     att, gq, gk, gv = pl.pallas_call(
         functools.partial(kernel, n, back),
@@ -259,9 +311,12 @@
             jax.ShapeDtypeStruct((tok, head_dim), jnp.float32),
             jax.ShapeDtypeStruct((tok, head_dim), jnp.float32),
         ),
-        in_specs=[vmem, vmem, vmem, hbm, smem, vmem],
+        in_specs=[hbm] * 6,
         out_specs=(hbm, hbm, vmem, vmem),
         scratch_shapes=[
+            pltpu.VMEM((tok, width), jnp.bfloat16),
+            pltpu.SMEM(lengths.shape, jnp.int32),
+            pltpu.VMEM(send_order.shape, jnp.int32),
             pltpu.VMEM((window, head_dim), jnp.bfloat16),
             pltpu.VMEM((window, head_dim), jnp.bfloat16),
             pltpu.VMEM((n, group, width), jnp.bfloat16),
@@ -277,27 +332,39 @@
             dma((2, back)),
             dma((n,)),
             dma((n,)),
-            dma((n,)),
-            dma((n,)),
-            dma((n,)),
-            dma((n,)),
+            dma((parts, n)),
+            dma((parts, n)),
+            dma((parts, n)),
+            dma((parts, n)),
             dma((2, back)),
             dma((2, back)),
-            dma((3,)),
+            dma((8,)),
         ],
         compiler_params=pltpu.CompilerParams(
-            collective_id=0, has_side_effects=True, vmem_limit_bytes=48 * 1024 * 1024
+            collective_id=0, has_side_effects=True, vmem_limit_bytes=vmem_limit
         ),
         cost_estimate=pl.CostEstimate(
             flops=flops, bytes_accessed=6 * tok * width, transcendentals=tok * heads * window
         ),
     )(queries, keys, values, grad_out.reshape(n, group, width), lengths, send_order)
-    return (
-        att.reshape(tok, width).astype(jnp.float32),
-        gq.reshape(tok, width).astype(jnp.float32),
-        gk,
-        gv,
-    )
+    steps = 2
+    wide = pl.BlockSpec((n // steps, group, width), lambda i: (i, 0, 0))
+    narrow = pl.BlockSpec((tok // steps, head_dim), lambda i: (i, 0))
+    blocks = (wide, wide, narrow, narrow)
+    att, gq, gk, gv = pl.pallas_call(
+        widen,
+        out_shape=(
+            jax.ShapeDtypeStruct((n, group, width), jnp.float32),
+            jax.ShapeDtypeStruct((n, group, width), jnp.float32),
+            jax.ShapeDtypeStruct((tok, head_dim), jnp.float32),
+            jax.ShapeDtypeStruct((tok, head_dim), jnp.float32),
+        ),
+        grid=(steps,),
+        in_specs=blocks,
+        out_specs=blocks,
+        compiler_params=pltpu.CompilerParams(vmem_limit_bytes=vmem_limit),
+    )(att, gq, gk, gv)
+    return (att.reshape(tok, width), gq.reshape(tok, width), gk, gv)
 
 
 def solution(mesh):

time: 38.4 us -> 33.6 us (0.88)
  local copies, waits for them, and re-layouts: 6.23 us -> 0 us
  Pallas kernels: 30.1 us -> 32.8 us
  other arithmetic: 1.13 us -> 0 us
    unnamed x14 -> x0, local copies, waits for them, and re-layouts: 6.23 us -> none
    pallas_call x0 -> x1, Pallas kernels: none -> 2.11 us  [per_device(): pl.pallas_call(widen, out_shape=(jax.ShapeDtypeStruct((n, group, width),...]
    convert_element_type x1 -> x0, other arithmetic: 1.13 us -> none  [per_device(): gq.reshape(tok, width).astype(jnp.float32)]
    pallas_call x1, Pallas kernels: 30.1 us -> 30.7 us  [per_device(): pl.pallas_call(functools.partial(kernel, n, back), out_shape=(jax.ShapeDt...]
where the time goes in v2:
time: 33.6 us; the launch traced here: 33.5 us
  Pallas kernels  32.8 us (98%)
  between operations  0.64 us (2%)
    pallas_call x1, Pallas kernels, per_device(): pl.pallas_call(functools.partial(kernel, n, back), out_shape=(jax.ShapeDt...  30.7 us
    pallas_call x1, Pallas kernels, per_device(): pl.pallas_call(widen, out_shape=(jax.ShapeDtypeStruct((n, group, width),...  2.11 us

profile of v2, /device:TPU:0, one launch (start us, length us, event | category | flops | bytes accessed | tf_op | source)
XLA Modules:
  0.0 33.5 jit_solution(16338336749886155821)
XLA Ops:
  0.6 30.7 %shard_map.93 = (bf16[8,32,512]{2,1,0:T(8,128)(2,1)}, bf16[8,32,512]{2,1,0:T(8,128)(2,1)}, f32[256,128]{1,0:T(8,128)}, f32[256,128]{1,0:T(8,128)}) custom-call(bf16[256,512]{1,0:T(8,128)(2,1)} %q_hbm.1, bf16[256,128]{1,0:T(8,128)(2,1)} %k_ref.1, bf16[256,128]{1,0:T(8,128)(2,1)} %v_ref.1, bf16[8,32,512]{2,1,0:T(8,128)(2,1)} %bitcast.5, s32[16]{0:T(128)} %len_hbm.1, ...), custom_call_target="tpu_custom_call" | custom-call | flops 1006632960 | bytes 786432 | tf_op jit(solution)/shard_map/pallas_call | solution.py:306
  31.4 2.1 %shard_map.94 = (f32[8,32,512]{2,1,0:T(8,128)}, f32[8,32,512]{2,1,0:T(8,128)}, f32[256,128]{1,0:T(8,128)}, f32[256,128]{1,0:T(8,128)}) custom-call(bf16[8,32,512]{2,1,0:T(8,128)(2,1)} %get-tuple-element.12.att_ref, bf16[8,32,512]{2,1,0:T(8,128)(2,1)} %get-tuple-element.13.gq_ref, f32[256,128]{1,0:T(8,128)} %get-tuple-element.14.gk_ref, ...), custom_call_target="tpu_custom_call" | custom-call | tf_op jit(solution)/shard_map/pallas_call | solution.py:354

commit v3 on v2

--- a/solution.py
+++ b/solution.py
@@ -80,16 +80,27 @@
             device_id_type=MESH,
         )
 
+    relay = back == 2 and n % 2 == 0
+    odd = lax.rem(me, 2)
+    partner = me + 1 - 2 * odd
+
     def halo_in(b):
         rows = pl.ds((back - b) * tok, tok)
-        target = peer(b)
+        target = partner if relay and b == 1 else peer(b)
         return (
             remote(k_ref, kwin.at[rows], kv_ssem.at[0, b - 1], kv_rsem.at[0, b - 1], target),
             remote(v_ref, vwin.at[rows], kv_ssem.at[1, b - 1], kv_rsem.at[1, b - 1], target),
         )
 
+    def halo_forward():
+        old, new = pl.ds(0, tok), pl.ds(tok, tok)
+        return (
+            remote(kwin.at[old], kwin.at[new], kv_ssem.at[0, 0], kv_rsem.at[0, 0], partner),
+            remote(vwin.at[old], vwin.at[new], kv_ssem.at[1, 0], kv_rsem.at[1, 0], partner),
+        )
+
     def halo_out(b):
-        target = peer(n - b)
+        target = partner if relay and b == 1 else peer(n - b)
         return (
             remote(
                 gk_send.at[b - 1],
@@ -148,9 +159,9 @@
             vwin[(back - b) * tok : (back - b + 1) * tok, :] = jnp.zeros((tok, head_dim), vwin.dtype)
 
     pl.semaphore_wait(barrier, n - 1)
-    for b in range(1, back + 1):
-
-        @pl.when(me + b < n)
+    for b in range(back, 0, -1):
+
+        @pl.when((odd == 0) if relay and b == 1 else (me + b < n))
         def _():
             for copy in halo_in(b):
                 copy.start()
@@ -177,9 +188,20 @@
     allowed = (key_pos >= start) & (key_pos <= query_pos)
     bias[...] = jnp.where(allowed, 0.0, masked_value)
 
+    if relay:
+
+        @pl.when(me >= 2)
+        def _():
+            for copy, onward in zip(halo_in(2), halo_forward()):
+                copy.wait_recv()
+
+                @pl.when(odd == 1)
+                def _():
+                    onward.start()
+
     for b in range(1, back + 1):
 
-        @pl.when(me + b < n)
+        @pl.when((odd == 0) if relay and b == 1 else (me + b < n))
         def _():
             for copy in halo_in(b):
                 copy.wait_send()
@@ -190,7 +212,7 @@
         def _():
             spread(g_ref, gbuf, g_ssem, g_rsem, offset).start()
 
-    for b in range(1, back + 1):
+    for b in range(1, 2 if relay else back + 1):
 
         @pl.when(me >= b)
         def _():
@@ -225,48 +247,78 @@
     for offset in range(1, n):
         spread(g_ref, gbuf, g_ssem, g_rsem, offset).wait_recv()
 
-    key_sum = None
+    def send_query_grads(part):
+        for h in range(part * heads // parts, (part + 1) * heads // parts):
+            query_grad = (dot_nn(key_t, score_grads[h]) * scale).T
+            cols = slice(h * head_dim, (h + 1) * head_dim)
+            gq_buf[:, :, cols] = query_grad.reshape(n, group, head_dim).astype(jnp.bfloat16)
+        for offset in range(1, n):
+            spread_part(gq_buf, gq_ref, gq_ssem, gq_rsem, part, offset).start()
+
+    score_grads = []
     for h in range(heads):
         cols = slice(h * head_dim, (h + 1) * head_dim)
         grad_float = gbuf[:, :, cols].astype(jnp.float32).reshape(tok, head_dim)
         grad = grad_float.astype(jnp.bfloat16)
         out_dot = jnp.sum(grad_float.T * att_cols[h], axis=0, keepdims=True)
         weight = weights[h]
-        score_grads = (weight * (dot_nt(value_all, grad) - out_dot)).astype(jnp.bfloat16)
-        query_grad = (dot_nn(key_t, score_grads) * scale).T
-        gq_buf[:, :, cols] = query_grad.reshape(n, group, head_dim).astype(jnp.bfloat16)
-        part = (h + 1) * parts // heads - 1
-        if (h + 1) * parts % heads == 0:
-            for offset in range(1, n):
-                spread_part(gq_buf, gq_ref, gq_ssem, gq_rsem, part, offset).start()
-        key_term = dot_nn(score_grads, picked[:, cols])
+        score_grads.append((weight * (dot_nt(value_all, grad) - out_dot)).astype(jnp.bfloat16))
+        key_term = dot_nn(score_grads[h], picked[:, cols])
         value_term = dot_nn(weight.astype(jnp.bfloat16), grad)
-        key_sum = key_term if key_sum is None else key_sum + key_term
+        key_sum = key_term if h == 0 else key_sum + key_term
         value_sum = value_term if h == 0 else value_sum + value_term
+        if h + 1 < heads and (h + 1) * parts % heads == 0:
+            send_query_grads((h + 1) * parts // heads - 1)
 
     key_sum = key_sum * scale
+
+    def add_landed(b):
+        gk_ref[...] += gk_land[b - 1].astype(jnp.float32)
+        gv_ref[...] += gv_land[b - 1].astype(jnp.float32)
+
     for b in range(1, back + 1):
         rows = slice((back - b) * tok, (back - b + 1) * tok)
         gk_send[b - 1] = key_sum[rows, :].astype(jnp.bfloat16)
         gv_send[b - 1] = value_sum[rows, :].astype(jnp.bfloat16)
 
-        @pl.when(me >= b)
+        @pl.when((me >= b) & (odd == 0) if relay and b == 2 else (me >= b))
         def _():
             for copy in halo_out(b):
                 copy.start()
 
+    gk_ref[...] = key_sum[back * tok :, :]
+    gv_ref[...] = value_sum[back * tok :, :]
+    send_query_grads(parts - 1)
     own_gq = pltpu.make_async_copy(gq_buf.at[me], gq_ref.at[me], own_sem.at[7])
     own_gq.start()
-    gk_ref[...] = key_sum[back * tok :, :]
-    gv_ref[...] = value_sum[back * tok :, :]
-    for b in range(1, back + 1):
+    if relay:
+
+        @pl.when((odd == 1) & (me >= 2))
+        def _():
+            for copy in halo_out(1):
+                copy.wait_recv()
+            gk_send[1] = (key_sum[:tok, :] + gk_land[0].astype(jnp.float32)).astype(jnp.bfloat16)
+            gv_send[1] = (value_sum[:tok, :] + gv_land[0].astype(jnp.float32)).astype(jnp.bfloat16)
+            for copy in halo_out(2):
+                copy.start()
+            for copy in halo_forward():
+                copy.wait_send()
+
+        @pl.when(odd == 0)
+        def _():
+            for copy in halo_out(1):
+                copy.wait_recv()
+            add_landed(1)
+
+    for b in range(2 if relay else 1, back + 1):
 
         @pl.when(me + b < n)
         def _():
             for copy in halo_out(b):
                 copy.wait_recv()
-            gk_ref[...] += gk_land[b - 1].astype(jnp.float32)
-            gv_ref[...] += gv_land[b - 1].astype(jnp.float32)
+            add_landed(b)
+
+    for b in range(1, back + 1):
 
         @pl.when(me >= b)
         def _():

time: 33.6 us -> 33.9 us (level)
  no operation moved by 1% of the time
where the time goes in v3:
time: 33.9 us; the launch traced here: 33.8 us
  Pallas kernels  33.1 us (98%)
  between operations  0.64 us (2%)
    pallas_call x1, Pallas kernels, per_device(): pl.pallas_call(functools.partial(kernel, n, back), out_shape=(jax.ShapeDt...  31 us
    pallas_call x1, Pallas kernels, per_device(): pl.pallas_call(widen, out_shape=(jax.ShapeDtypeStruct((n, group, width),...  2.11 us

profile of v3, /device:TPU:0, one launch (start us, length us, event | category | flops | bytes accessed | tf_op | source)
XLA Modules:
  0.0 33.8 jit_solution(2994568466162852947)
XLA Ops:
  0.6 31.0 %shard_map.93 = (bf16[8,32,512]{2,1,0:T(8,128)(2,1)}, bf16[8,32,512]{2,1,0:T(8,128)(2,1)}, f32[256,128]{1,0:T(8,128)}, f32[256,128]{1,0:T(8,128)}) custom-call(bf16[256,512]{1,0:T(8,128)(2,1)} %q_hbm.1, bf16[256,128]{1,0:T(8,128)(2,1)} %k_ref.1, bf16[256,128]{1,0:T(8,128)(2,1)} %v_ref.1, bf16[8,32,512]{2,1,0:T(8,128)(2,1)} %bitcast.5, s32[16]{0:T(128)} %len_hbm.1, ...), custom_call_target="tpu_custom_call" | custom-call | flops 1006632960 | bytes 786432 | tf_op jit(solution)/shard_map/pallas_call | solution.py:358
  31.7 2.1 %shard_map.94 = (f32[8,32,512]{2,1,0:T(8,128)}, f32[8,32,512]{2,1,0:T(8,128)}, f32[256,128]{1,0:T(8,128)}, f32[256,128]{1,0:T(8,128)}) custom-call(bf16[8,32,512]{2,1,0:T(8,128)(2,1)} %get-tuple-element.12.att_ref, bf16[8,32,512]{2,1,0:T(8,128)(2,1)} %get-tuple-element.13.gq_ref, f32[256,128]{1,0:T(8,128)} %get-tuple-element.14.gk_ref, ...), custom_call_target="tpu_custom_call" | custom-call | tf_op jit(solution)/shard_map/pallas_call | solution.py:406

commit v4 on v3

--- a/solution.py
+++ b/solution.py
@@ -124,15 +124,15 @@
 
     def spread_part(src, dst, ssem, rsem, part, offset):
         target = peer(offset)
-        width = heads // parts * head_dim
-        cols = pl.ds(part * width, width)
         return remote(
-            src.at[target, :, cols],
-            dst.at[me, :, cols],
+            src.at[part, target],
+            dst.at[part, me],
             ssem.at[part, offset],
             rsem.at[part, offset],
             target,
         )
+
+    far_first = sorted(range(1, n), key=lambda offset: abs(offset - n // 2))
 
     barrier = pltpu.get_barrier_semaphore()
     for offset in range(1, n):
@@ -166,11 +166,8 @@
             for copy in halo_in(b):
                 copy.start()
 
-    for offset in range(1, n):
-
-        @pl.when(peer(offset) < me)
-        def _():
-            spread(g_ref, gbuf, g_ssem, g_rsem, offset).start()
+    for offset in far_first:
+        spread(g_ref, gbuf, g_ssem, g_rsem, offset).start()
 
     for copy in local:
         copy.wait()
@@ -199,19 +196,6 @@
                 def _():
                     onward.start()
 
-    for b in range(1, back + 1):
-
-        @pl.when((odd == 0) if relay and b == 1 else (me + b < n))
-        def _():
-            for copy in halo_in(b):
-                copy.wait_send()
-
-    for offset in range(1, n):
-
-        @pl.when(peer(offset) > me)
-        def _():
-            spread(g_ref, gbuf, g_ssem, g_rsem, offset).start()
-
     for b in range(1, 2 if relay else back + 1):
 
         @pl.when(me >= b)
@@ -236,12 +220,13 @@
         att_t = dot_nn(value_t, weight.astype(jnp.bfloat16))
         att_low = att_t.T
         att_cols.append(att_t.astype(jnp.bfloat16).astype(jnp.float32))
-        att_buf[:, :, cols] = att_low.reshape(n, group, head_dim).astype(jnp.bfloat16)
-        part = (h + 1) * parts // heads - 1
+        part, place = divmod(h, heads // parts)
+        part_cols = slice(place * head_dim, (place + 1) * head_dim)
+        att_buf[part, :, :, part_cols] = att_low.reshape(n, group, head_dim).astype(jnp.bfloat16)
         if (h + 1) * parts % heads == 0:
-            for offset in range(1, n):
+            for offset in far_first:
                 spread_part(att_buf, att_ref, a_ssem, a_rsem, part, offset).start()
-    own_att = pltpu.make_async_copy(att_buf.at[me], att_ref.at[me], own_sem.at[6])
+    own_att = pltpu.make_async_copy(att_buf.at[:, me], att_ref.at[:, me], own_sem.at[6])
     own_att.start()
 
     for offset in range(1, n):
@@ -250,9 +235,10 @@
     def send_query_grads(part):
         for h in range(part * heads // parts, (part + 1) * heads // parts):
             query_grad = (dot_nn(key_t, score_grads[h]) * scale).T
-            cols = slice(h * head_dim, (h + 1) * head_dim)
-            gq_buf[:, :, cols] = query_grad.reshape(n, group, head_dim).astype(jnp.bfloat16)
-        for offset in range(1, n):
+            place = h % (heads // parts)
+            part_cols = slice(place * head_dim, (place + 1) * head_dim)
+            gq_buf[part, :, :, part_cols] = query_grad.reshape(n, group, head_dim).astype(jnp.bfloat16)
+        for offset in far_first:
             spread_part(gq_buf, gq_ref, gq_ssem, gq_rsem, part, offset).start()
 
     score_grads = []
@@ -289,7 +275,7 @@
     gk_ref[...] = key_sum[back * tok :, :]
     gv_ref[...] = value_sum[back * tok :, :]
     send_query_grads(parts - 1)
-    own_gq = pltpu.make_async_copy(gq_buf.at[me], gq_ref.at[me], own_sem.at[7])
+    own_gq = pltpu.make_async_copy(gq_buf.at[:, me], gq_ref.at[:, me], own_sem.at[7])
     own_gq.start()
     if relay:
 
@@ -325,6 +311,13 @@
             for copy in halo_out(b):
                 copy.wait_send()
 
+    for b in range(1, back + 1):
+
+        @pl.when((odd == 0) if relay and b == 1 else (me + b < n))
+        def _():
+            for copy in halo_in(b):
+                copy.wait_send()
+
     own_att.wait()
     own_gq.wait()
     for offset in range(1, n):
@@ -335,8 +328,11 @@
 
 
 def widen(att_ref, gq_ref, gk_ref, gv_ref, att_out, gq_out, gk_out, gv_out):
-    att_out[...] = att_ref[...].astype(jnp.float32)
-    gq_out[...] = gq_ref[...].astype(jnp.float32)
+    parts, _, _, width = att_ref.shape
+    for part in range(parts):
+        cols = slice(part * width, (part + 1) * width)
+        att_out[:, :, cols] = att_ref[part].astype(jnp.float32)
+        gq_out[:, :, cols] = gq_ref[part].astype(jnp.float32)
     gk_out[...] = gk_ref[...]
     gv_out[...] = gv_ref[...]
 
@@ -358,8 +354,8 @@
     att, gq, gk, gv = pl.pallas_call(
         functools.partial(kernel, n, back),
         out_shape=(
-            jax.ShapeDtypeStruct((n, group, width), jnp.bfloat16),
-            jax.ShapeDtypeStruct((n, group, width), jnp.bfloat16),
+            jax.ShapeDtypeStruct((parts, n, group, width // parts), jnp.bfloat16),
+            jax.ShapeDtypeStruct((parts, n, group, width // parts), jnp.bfloat16),
             jax.ShapeDtypeStruct((tok, head_dim), jnp.float32),
             jax.ShapeDtypeStruct((tok, head_dim), jnp.float32),
         ),
@@ -372,8 +368,8 @@
             pltpu.VMEM((window, head_dim), jnp.bfloat16),
             pltpu.VMEM((window, head_dim), jnp.bfloat16),
             pltpu.VMEM((n, group, width), jnp.bfloat16),
-            pltpu.VMEM((n, group, width), jnp.bfloat16),
-            pltpu.VMEM((n, group, width), jnp.bfloat16),
+            pltpu.VMEM((parts, n, group, width // parts), jnp.bfloat16),
+            pltpu.VMEM((parts, n, group, width // parts), jnp.bfloat16),
             pltpu.VMEM((window, tok), jnp.float32),
             pltpu.VMEM((heads, window, tok), jnp.float32),
             pltpu.VMEM((back, tok, head_dim), jnp.bfloat16),
@@ -402,7 +398,7 @@
     steps = 2
     wide = pl.BlockSpec((n // steps, group, width), lambda i: (i, 0, 0))
     narrow = pl.BlockSpec((tok // steps, head_dim), lambda i: (i, 0))
-    blocks = (wide, wide, narrow, narrow)
+    halves = pl.BlockSpec((parts, n // steps, group, width // parts), lambda i: (0, i, 0, 0))
     att, gq, gk, gv = pl.pallas_call(
         widen,
         out_shape=(
@@ -412,8 +408,8 @@
             jax.ShapeDtypeStruct((tok, head_dim), jnp.float32),
         ),
         grid=(steps,),
-        in_specs=blocks,
-        out_specs=blocks,
+        in_specs=(halves, halves, narrow, narrow),
+        out_specs=(wide, wide, narrow, narrow),
         compiler_params=pltpu.CompilerParams(vmem_limit_bytes=vmem_limit),
     )(att, gq, gk, gv)
     return (att.reshape(tok, width), gq.reshape(tok, width), gk, gv)

time: 33.9 us -> 33.6 us (level)
    pallas_call x1, Pallas kernels: 31 us -> 30.7 us  [per_device(): pl.pallas_call(functools.partial(kernel, n, back), out_shape=(jax.ShapeDt...]
where the time goes in v4:
time: 33.6 us; the launch traced here: 33.4 us
  Pallas kernels  32.8 us (98%)
  between operations  0.64 us (2%)
    pallas_call x1, Pallas kernels, per_device(): pl.pallas_call(functools.partial(kernel, n, back), out_shape=(jax.ShapeDt...  30.7 us
    pallas_call x1, Pallas kernels, per_device(): pl.pallas_call(widen, out_shape=(jax.ShapeDtypeStruct((n, group, width),...  2.11 us

profile of v4, /device:TPU:0, one launch (start us, length us, event | category | flops | bytes accessed | tf_op | source)
XLA Modules:
  0.0 33.4 jit_solution(16328279744826074945)
XLA Ops:
  0.6 30.7 %shard_map.93 = (bf16[2,8,32,256]{3,2,1,0:T(8,128)(2,1)}, bf16[2,8,32,256]{3,2,1,0:T(8,128)(2,1)}, f32[256,128]{1,0:T(8,128)}, f32[256,128]{1,0:T(8,128)}) custom-call(bf16[256,512]{1,0:T(8,128)(2,1)} %q_hbm.1, bf16[256,128]{1,0:T(8,128)(2,1)} %k_ref.1, bf16[256,128]{1,0:T(8,128)(2,1)} %v_ref.1, bf16[8,32,512]{2,1,0:T(8,128)(2,1)} %bitcast.5, s32[16]{0:T(128)} %len_hbm.1, ...), custom_call_target="tpu_custom_call" | custom-call | flops 1006632960 | bytes 786432 | tf_op jit(solution)/shard_map/pallas_call | solution.py:354
  31.3 2.1 %shard_map.94 = (f32[8,32,512]{2,1,0:T(8,128)}, f32[8,32,512]{2,1,0:T(8,128)}, f32[256,128]{1,0:T(8,128)}, f32[256,128]{1,0:T(8,128)}) custom-call(bf16[2,8,32,256]{3,2,1,0:T(8,128)(2,1)} %get-tuple-element.12.att_ref, bf16[2,8,32,256]{3,2,1,0:T(8,128)(2,1)} %get-tuple-element.13.gq_ref, f32[256,128]{1,0:T(8,128)} %get-tuple-element.14.gk_ref, ...), custom_call_target="tpu_custom_call" | custom-call | tf_op jit(solution)/shard_map/pallas_call | solution.py:402

commit v5 on v4

--- a/solution.py
+++ b/solution.py
@@ -185,6 +185,15 @@
     allowed = (key_pos >= start) & (key_pos <= query_pos)
     bias[...] = jnp.where(allowed, 0.0, masked_value)
 
+    def score_rows(b):
+        rows = slice((back - b) * tok, (back - b + 1) * tok)
+        block = kwin[rows, :]
+        for h in range(heads):
+            cols = slice(h * head_dim, (h + 1) * head_dim)
+            weights[h, rows, :] = dot_nt(block, picked[:, cols]) + bias[rows, :]
+        return vwin[rows, :].astype(jnp.float32).T.astype(jnp.bfloat16)
+
+    value_blocks = {0: score_rows(0)}
     if relay:
 
         @pl.when(me >= 2)
@@ -196,6 +205,8 @@
                 def _():
                     onward.start()
 
+        value_blocks[2] = score_rows(2)
+
     for b in range(1, 2 if relay else back + 1):
 
         @pl.when(me >= b)
@@ -203,16 +214,14 @@
             for copy in halo_in(b):
                 copy.wait_recv()
 
-    key_all = kwin[...]
-    value_all = vwin[...]
-    key_t = key_all.astype(jnp.float32).T.astype(jnp.bfloat16)
-    value_t = value_all.astype(jnp.float32).T.astype(jnp.bfloat16)
+        value_blocks[b] = score_rows(b)
+
+    value_t = jnp.concatenate([value_blocks[b] for b in range(back, -1, -1)], axis=1)
     exponent = scale * math.log2(math.e)
 
     att_cols = []
     for h in range(heads):
-        cols = slice(h * head_dim, (h + 1) * head_dim)
-        scores = dot_nt(key_all, picked[:, cols]) + bias[...]
+        scores = weights[h]
         row_max = jnp.max(scores, axis=0, keepdims=True)
         exps = jnp.exp2((scores - row_max) * exponent)
         weight = exps * (1.0 / jnp.sum(exps, axis=0, keepdims=True))
@@ -228,6 +237,8 @@
                 spread_part(att_buf, att_ref, a_ssem, a_rsem, part, offset).start()
     own_att = pltpu.make_async_copy(att_buf.at[:, me], att_ref.at[:, me], own_sem.at[6])
     own_att.start()
+    key_t = kwin[...].astype(jnp.float32).T.astype(jnp.bfloat16)
+    value_all = vwin[...]
 
     for offset in range(1, n):
         spread(g_ref, gbuf, g_ssem, g_rsem, offset).wait_recv()

time: 33.6 us -> 33.1 us (0.985)
  Pallas kernels: 32.8 us -> 32.3 us
    pallas_call x1, Pallas kernels: 30.7 us -> 30.2 us  [per_device(): pl.pallas_call(functools.partial(kernel, n, back), out_shape=(jax.ShapeDt...]
where the time goes in v5:
time: 33.1 us; the launch traced here: 32.9 us
  Pallas kernels  32.3 us (98%)
  between operations  0.64 us (2%)
    pallas_call x1, Pallas kernels, per_device(): pl.pallas_call(functools.partial(kernel, n, back), out_shape=(jax.ShapeDt...  30.2 us
    pallas_call x1, Pallas kernels, per_device(): pl.pallas_call(widen, out_shape=(jax.ShapeDtypeStruct((n, group, width),...  2.11 us

profile of v5, /device:TPU:0, one launch (start us, length us, event | category | flops | bytes accessed | tf_op | source)
XLA Modules:
  0.0 32.9 jit_solution(2363276838163323396)
XLA Ops:
  0.6 30.2 %shard_map.93 = (bf16[2,8,32,256]{3,2,1,0:T(8,128)(2,1)}, bf16[2,8,32,256]{3,2,1,0:T(8,128)(2,1)}, f32[256,128]{1,0:T(8,128)}, f32[256,128]{1,0:T(8,128)}) custom-call(bf16[256,512]{1,0:T(8,128)(2,1)} %q_hbm.1, bf16[256,128]{1,0:T(8,128)(2,1)} %k_ref.1, bf16[256,128]{1,0:T(8,128)(2,1)} %v_ref.1, bf16[8,32,512]{2,1,0:T(8,128)(2,1)} %bitcast.5, s32[16]{0:T(128)} %len_hbm.1, ...), custom_call_target="tpu_custom_call" | custom-call | flops 1006632960 | bytes 786432 | tf_op jit(solution)/shard_map/pallas_call | solution.py:365
  30.8 2.1 %shard_map.94 = (f32[8,32,512]{2,1,0:T(8,128)}, f32[8,32,512]{2,1,0:T(8,128)}, f32[256,128]{1,0:T(8,128)}, f32[256,128]{1,0:T(8,128)}) custom-call(bf16[2,8,32,256]{3,2,1,0:T(8,128)(2,1)} %get-tuple-element.12.att_ref, bf16[2,8,32,256]{3,2,1,0:T(8,128)(2,1)} %get-tuple-element.13.gq_ref, f32[256,128]{1,0:T(8,128)} %get-tuple-element.14.gk_ref, ...), custom_call_target="tpu_custom_call" | custom-call | tf_op jit(solution)/shard_map/pallas_call | solution.py:413
